TPU v7x, 128 devices: a whole 4x4x4 slice. The times are simulated.
128 devices in a mesh: row: 16 (over x_hi, z, core), col: 8 (over x_lo, y).
Axes of the slice: x: 4 (x_hi: 2, x_lo: 2; x = x_hi * 2 + x_lo), y: 4, z: 4, core: 2. Of those that a mesh axis runs over, the one named last changes fastest.
Arguments:
- sign_iterate: float32 [6144, 6144], P('row', 'col'), may hold values from -1.25 to 1.25
- operand_pattern: int32 [1024, 1024], P('row', 'col'), may hold values from 0 to 1, as said below
- product_pattern: int32 [1024, 1024], P('row', 'col'), may hold values from 0 to 1, as said below
Outputs:
- sign_next: float32 [6144, 6144], P('row', 'col')
- defect: float32 [], replicated
Inputs may be any that keep to these rules, and one draw needn't show every extreme that they name: `operand_pattern`: symmetric, 1 on the diagonal. `product_pattern`: symmetric, 1 on the diagonal and wherever operand_pattern is 1.
All inputs are finite; a program needn't handle non-finite values.
Results may differ from a plain program's by a relative error of at most 0.000076.
Values sent between devices are 32-bit elements; how exact they have to be, the bound alone decides.
No kernel may reach another device: no remote copies, remote signals or barrier semaphores. Data moves between devices by JAX's collectives and lax.ppermute only.
A program may use at most 128 MiB of HBM per device.

v0:
```python
import jax
import jax.numpy as jnp
from jax import lax
from jax.sharding import PartitionSpec as P

BS = 6


def expand_blocks(pattern, row_first, col_first):
    count_rows, count_cols = pattern.shape
    block_rows = row_first + jnp.arange(count_rows, dtype=jnp.int32)
    block_cols = col_first + jnp.arange(count_cols, dtype=jnp.int32)
    on_diagonal = block_rows[:, None] == block_cols[None, :]
    forced = jnp.where(on_diagonal, 1, pattern).astype(jnp.float32)
    wide = jnp.broadcast_to(forced[:, None, :, None], (count_rows, BS, count_cols, BS))
    return wide.reshape(count_rows * BS, count_cols * BS)


def matmul_high(left, right):
    return jnp.dot(left, right, precision=lax.Precision.HIGHEST, preferred_element_type=jnp.float32)


def per_device(sign_iterate, operand_pattern, product_pattern):
    local_rows, local_cols = sign_iterate.shape
    row_first = lax.axis_index("row") * operand_pattern.shape[0]
    col_first = lax.axis_index("col") * operand_pattern.shape[1]
    operand_mask = expand_blocks(operand_pattern, row_first, col_first)
    product_mask = expand_blocks(product_pattern, row_first, col_first)
    sparse_iterate = sign_iterate * operand_mask
    entry_rows = row_first * BS + jnp.arange(local_rows, dtype=jnp.int32)
    entry_cols = col_first * BS + jnp.arange(local_cols, dtype=jnp.int32)
    identity = (entry_rows[:, None] == entry_cols[None, :]).astype(jnp.float32)

    def product(left_part, right_part):
        column_block = lax.all_gather(right_part, "row", axis=0, tiled=True)
        return matmul_high(lax.all_gather(left_part, "col", axis=1, tiled=True), column_block)

    square = product(sparse_iterate, sparse_iterate) * product_mask
    polynomial = 3.0 * identity - square
    sign_next = 0.5 * product(sparse_iterate, polynomial) * product_mask
    local_defect = jnp.sum((square - identity) ** 2)
    defect = lax.psum(local_defect, ("row", "col"))
    return (sign_next, defect)


def solution(mesh):
    in_specs = (P("row", "col"), P("row", "col"), P("row", "col"))
    out_specs = (P("row", "col"), P())
    return jax.shard_map(
        per_device, mesh=mesh, in_specs=in_specs, out_specs=out_specs, check_vma=False
    )
```

profile of v0, /device:TPU:1, one launch (start us, length us, event | category | flops | bytes accessed | tf_op | source)
XLA Modules:
  0.0 447.6 jit_solution(4580253689497543570)
XLA Ops:
  7.2 0.0 all-gather.4.cloned.1.call-start
  7.2 0.9 fusion.5
  8.1 11.6 %broadcast_in_dim.10 = f32[64,6,128,6]{3,2,1,0:T(8,128)} broadcast(f32[64,128]{1,0:T(8,128)S(1)} %get-tuple-element.4), dimensions={0,2} | broadcast | bytes 1212416 | tf_op jit(solution)/shard_map/broadcast_in_dim | solution.py:15
  19.7 0.0 copy-start
  19.7 18.5 %reshape.28 = f32[384,768]{1,0:T(8,128)S(1)} reshape(f32[64,6,128,6]{3,2,1,0:T(8,128)} %broadcast_in_dim.10) | data formatting | bytes 2359296 | tf_op jit(solution)/shard_map/reshape | solution.py:16
  38.2 0.0 copy-done
  38.2 1.1 mul.35
  39.3 0.0 all-gather.4.cloned.1.call-update
  39.4 0.0 all-gather.6.cloned.1.call-start
  39.4 0.7 all-gather.6.cloned.1.call-update
  40.1 0.2 all-gather.8.cloned.1.call-start
  40.3 11.9 %broadcast_in_dim.11 = f32[64,6,128,6]{3,2,1,0:T(8,128)} broadcast(f32[64,128]{1,0:T(8,128)S(1)} %get-tuple-element.5), dimensions={0,2} | broadcast | bytes 1212416 | tf_op jit(solution)/shard_map/broadcast_in_dim | solution.py:15
  52.3 18.5 %reshape.29 = f32[384,768]{1,0:T(8,128)S(1)} reshape(f32[64,6,128,6]{3,2,1,0:T(8,128)} %broadcast_in_dim.11) | data formatting | bytes 2359296 | tf_op jit(solution)/shard_map/reshape | solution.py:16
  70.8 73.6 %all-gather.4.cloned.1.call-done = f32[384,6144]{1,0:T(8,128)} async-done(((f32[384,768]{1,0:T(8,128)}), f32[384,6144]{1,0:T(8,128)}) %all-gather.4.cloned.1.call-update) | async-done | bytes 9437200 | tf_op jit(solution)/shard_map/all_gather | solution.py:36
  144.4 121.3 %all-gather.6.cloned.1.call-done = f32[6144,768]{1,0:T(8,128)} async-done(((f32[384,768]{1,0:T(8,128)}), f32[6144,768]{1,0:T(8,128)}) %all-gather.6.cloned.1.call-update) | async-done | bytes 18874384 | tf_op jit(solution)/shard_map/all_gather | solution.py:35
  265.7 29.1 %fusion.4 = (f32[]{:T(128)}, f32[384,768]{1,0:T(8,128)}) fusion(s32[768]{0:T(1024)S(1)} %iota_add_fusion, s32[384]{0:T(512)S(1)} %iota_add_fusion.1, f32[384,768]{1,0:T(8,128)S(1)} %reshape.29, f32[384,6144]{1,0:T(8,128)} %all-gather.4.cloned.1.call-done, f32[6144,768]{1,0:T(8,128)} %all-gather.6.cloned.1.call-done), kind=kOutput, calls=%fused_computation.8 | convolution fusion | flops 21745631232 | bytes 30675460 | tf_op jit(solution)/shard_map/dot_general | solution.py:20
  294.9 0.0 all-gather.8.cloned.1.call-update
  294.9 101.6 %psum.7 = f32[]{:T(128)} all-reduce(f32[]{:T(128)} %get-tuple-element.2), channel_id=1, replica_groups=mesh['row'=16,'col'=8] {'row','col'}, use_global_device_ids=true, to_apply=%region_1.2 | all-reduce | flops 1 | bytes 8 | tf_op jit(solution)/shard_map/psum | solution.py:42
  396.5 16.5 %all-gather.8.cloned.1.call-done = f32[6144,768]{1,0:T(8,128)} async-done(((f32[384,768]{1,0:T(8,128)}), f32[6144,768]{1,0:T(8,128)}) %all-gather.8.cloned.1.call-update) | async-done | bytes 18874384 | tf_op jit(solution)/shard_map/all_gather | solution.py:35
  413.0 28.1 %fusion = f32[384,768]{1,0:T(8,128)} fusion(f32[384,768]{1,0:T(8,128)S(1)} %reshape.29, f32[384,6144]{1,0:T(8,128)} %all-gather.4.cloned.1.call-done, f32[6144,768]{1,0:T(8,128)} %all-gather.8.cloned.1.call-done), kind=kOutput, calls=%fused_computation.4 | convolution fusion | flops 21743861760 | bytes 30670848 | tf_op jit(solution)/shard_map/dot_general | solution.py:20
  (4 shorter events, 0.0 us)
Async XLA Ops:
  7.2 137.3 %all-gather.4.cloned.1.call-start = ((), (), s32[]{:S(2)}) async-start(), calls=%async_computation | async-start | bytes 10616832 | tf_op jit(solution)/shard_map/all_gather | solution.py:36
  19.7 18.5 %copy-start = (f32[384,768]{1,0:T(8,128)S(1)}, f32[384,768]{1,0:T(8,128)}, u32[]{:S(2)}) copy-start(f32[384,768]{1,0:T(8,128)} %param.3) | copy-start | bytes 3538948
  39.4 226.4 %all-gather.6.cloned.1.call-start = ((), (), s32[]{:S(2)}) async-start(), calls=%async_computation.1 | async-start | bytes 20054016 | tf_op jit(solution)/shard_map/all_gather | solution.py:35
  40.1 372.9 %all-gather.8.cloned.1.call-start = ((), (), s32[]{:S(2)}) async-start(), calls=%async_computation.2 | async-start | bytes 20054016 | tf_op jit(solution)/shard_map/all_gather | solution.py:35
Sparse Core Ops, SparseCore 0:
  39.5 104.9 all-gather.3
  147.5 118.2 all-gather.5
  295.0 117.9 all-gather.7
where the time goes:
time: 448 us
  waiting for transfers between devices  212 us (47%)
  blocking collectives  102 us (23%)
  local copies, waits for them, and re-layouts  60.5 us (14%)
  matrix products  57.2 us (13%)
  between operations  13.8 us (3%)
    all_gather x2, waiting for transfers between devices, product(): column_block = lax.all_gather(right_part, 'row', axis=0, tiled=True)  138 us
    psum x1, blocking collectives, per_device(): defect = lax.psum(local_defect, ('row', 'col'))  102 us
    all_gather x1, waiting for transfers between devices, product(): lax.all_gather(left_part, 'col', axis=1, tiled=True)  73.6 us
    dot_general x2, matrix products, matmul_high(): jnp.dot(left, right, precision=lax.Precision.HIGHEST, preferred_element_t...  57.2 us
    reshape x2, local copies, waits for them, and re-layouts, expand_blocks(): return wide.reshape(count_rows * BS, count_cols * BS)  37 us
    broadcast_in_dim x2, local copies, waits for them, and re-layouts, expand_blocks(): jnp.broadcast_to(forced[:, None, :, None], (count_rows, BS, count_cols, BS))  23.5 us
  transfers between devices with their start and end apart: 3, of which 3 were waited for; matrix products, arithmetic and copies ran while one was open for 7% of the time, Pallas kernels for 0%

commit v1 on v0

v1 whole, which is shorter than its diff:
```python
import functools

import jax
import jax.numpy as jnp
import numpy as np
from jax import lax
from jax.experimental import pallas as pl
from jax.experimental.pallas import tpu as pltpu
from jax.sharding import PartitionSpec as P

BS = 6
AXES = ("row", "col")
LANES = 128
FLAG = 1024.0
SLOTS_X = 42
SLOTS_S = 64
WIDE_X = 256
WIDE_S = 384
EXTRA = 8
VMEM = 56 * 1024 * 1024


def send(value, move):
    pairs = []
    for row in range(16):
        for col in range(8):
            here = (row // 8, row // 2 % 4, row % 2, col // 4, col % 4)
            xh, z, core, xl, y = move(*here)
            pairs.append((row * 8 + col, ((xh % 2) * 8 + (z % 4) * 2 + core % 2) * 8 + (xl % 2) * 4 + y % 4))
    return lax.ppermute(value, AXES, pairs)


def along(xh=0, z=0, core=0, xl=0, y=0):
    return lambda a, b, c, d, e: (a + xh, b + z, c + core, d + xl, e + y)


def tables():
    row_of = np.arange(64 * BS)[:, None] // BS == np.arange(64)[None, :]
    molecule = np.arange(LANES)[:, None]
    lane = np.arange(LANES * BS)[None, :] // BS
    place = BS * (molecule < lane) + FLAG * (molecule == lane)
    until = np.arange(LANES)[:, None] <= np.arange(LANES)[None, :]
    slot_x = BS * (np.arange(LANES)[:, None] == np.arange(WIDE_X)[None, :] // BS)
    slot_s = BS * (np.arange(LANES)[:, None] == np.arange(WIDE_S)[None, :] // BS)
    within = np.broadcast_to(np.arange(LANES * BS) % BS, (8, LANES * BS))
    to = lambda t: jnp.asarray(t.astype(np.float32), jnp.bfloat16)
    return to(row_of), to(place), to(until), to(slot_x), to(slot_s), jnp.asarray(within.astype(np.int32))


def dot(a, b):
    return jnp.dot(a, b, preferred_element_type=jnp.float32)


def take(source, index):
    return jnp.take_along_axis(source, index, axis=1, mode="promise_in_bounds")


def packed_columns(pattern, row_of, until, slot, within):
    bits = pattern.astype(jnp.bfloat16)
    count = dot(bits, until)
    wanted = lax.broadcasted_iota(jnp.int32, count.shape, 1).astype(jnp.float32)
    position = jnp.zeros(count.shape, jnp.int32)
    for step in (64, 32, 16, 8, 4, 2, 1):
        below = take(count, position + (step - 1)) <= wanted
        position = jnp.where(below, position + step, position)
    rows = dot(row_of, position.astype(jnp.float32).astype(jnp.bfloat16))
    width = slot.shape[1]
    columns = dot(rows.astype(jnp.bfloat16), slot).astype(jnp.int32) + within[0:1, :width]
    return columns, jnp.max(count[:, LANES - 1 :])


def pack_rows(source, columns, chunk, width):
    outs = []
    for j in range(width // LANES):
        index = columns[:, j * LANES : (j + 1) * LANES]
        low = index & (LANES - 1)
        high = index >> 7
        value = take(source(j), low)
        for k in range(j + 1, BS):
            value = jnp.where(high == k, take(source(k), low), value)
        outs.append(value)
    return outs


def pack_kernel(x_ref, pattern_ref, row_of_ref, until_ref, slot_ref, within_ref, out_ref, flag_ref, columns_ref):
    pattern = pattern_ref[...]
    columns, most = packed_columns(pattern, row_of_ref[...], until_ref[...], slot_ref[...], within_ref[...])
    columns_ref[...] = columns
    flag_ref[...] = jnp.full(flag_ref.shape, jnp.where(most > SLOTS_X, 1.0, 0.0), jnp.float32)

    def body(i, carry):
        rows = pl.ds(pl.multiple_of(i * 48, 48), 48)
        outs = pack_rows(lambda k: x_ref[rows, k * LANES : (k + 1) * LANES], columns_ref[rows, :], 48, WIDE_X)
        for j, value in enumerate(outs):
            out_ref[rows, j * LANES : (j + 1) * LANES] = value
        return carry

    lax.fori_loop(0, 8, body, 0)
    real = pattern.astype(jnp.float32)
    out_ref[384:416, :LANES] = real[:32]
    out_ref[384:416, LANES:] = real[32:]


def plan_kernel(pattern_ref, row_of_ref, until_ref, slot_ref, within_ref, columns_ref, flag_ref):
    columns, most = packed_columns(pattern_ref[...], row_of_ref[...], until_ref[...], slot_ref[...], within_ref[...])
    columns_ref[...] = columns
    flag_ref[...] = jnp.full(flag_ref.shape, jnp.where(most > SLOTS_S, 1.0, 0.0), jnp.float32)


def codes(pattern, row_of, place):
    rows = dot(row_of, pattern.astype(jnp.bfloat16)).astype(jnp.bfloat16)
    return dot(rows, place)


def unpack(packed_ref, code_ref, within_ref, high_ref, low_ref, width, first):
    def body(i, carry):
        rows = pl.ds(pl.multiple_of(i * 48, 48), 48)
        target = pl.ds(pl.multiple_of(first + i * 48, 48), 48)
        sources = [packed_ref[rows, k * LANES : (k + 1) * LANES] for k in range(width // LANES)]
        for j in range(BS):
            span = slice(j * LANES, (j + 1) * LANES)
            code = code_ref[rows, span]
            index = (code.astype(jnp.int32) + within_ref[0:1, span]) & 1023
            low = index & (LANES - 1)
            value = take(sources[0], low)
            for k in range(1, min(j + 1, len(sources))):
                value = jnp.where(index >= k * LANES, take(sources[k], low), value)
            value = jnp.where(code >= FLAG, value, 0.0)
            high = value.astype(jnp.bfloat16)
            high_ref[target, span] = high
            low_ref[target, span] = (value - high.astype(jnp.float32)).astype(jnp.bfloat16)
        return carry

    lax.fori_loop(0, 8, body, 0)


def carried_pattern(stack_ref, slot):
    return jnp.concatenate([stack_ref[slot, 384:416, :LANES], stack_ref[slot, 384:416, LANES:]], axis=0)


def left_kernel(where_ref, *refs):
    blocks = refs[:8]
    row_of_ref, place_ref, within_ref, high_ref, low_ref, stack_ref, code_ref, sems = refs[8:]
    step = pl.program_id(0)

    @pl.when(step == 0)
    def _():
        for k in range(8):
            pltpu.make_async_copy(blocks[k], stack_ref.at[k], sems.at[k]).start()

    pltpu.make_async_copy(blocks[0], stack_ref.at[step], sems.at[step]).wait()
    code_ref[...] = codes(carried_pattern(stack_ref, step), row_of_ref[...], place_ref[...])
    unpack(stack_ref.at[step], code_ref, within_ref, high_ref.at[0], low_ref.at[0], WIDE_X, 0)


def accumulate(step, left_high_ref, left_low_ref, high_ref, low_ref, total_ref):
    for j in range(3):
        span = slice(j * 256, (j + 1) * 256)
        part = dot(left_high_ref[0], high_ref[:, span]) + dot(left_high_ref[0], low_ref[:, span])
        part = part + dot(left_low_ref[0], high_ref[:, span])

        @pl.when(step == 0)
        def _():
            total_ref[:, span] = part

        @pl.when(step > 0)
        def _():
            total_ref[:, span] += part


def square_kernel(where_ref, *refs):
    blocks = refs[:16]
    left_high_ref, left_low_ref, pattern_ref, columns_ref, row_of_ref, place_ref, within_ref = refs[16:23]
    out_ref, defect_ref, stack_ref, code_ref, high_ref, low_ref, total_ref, sems = refs[23:]
    step = pl.program_id(0)

    @pl.when(step == 0)
    def _():
        for k in range(16):
            slot = where_ref[k]
            pltpu.make_async_copy(blocks[k], stack_ref.at[slot], sems.at[slot]).start()

    for half in range(2):
        slot = 2 * step + half
        pltpu.make_async_copy(blocks[0], stack_ref.at[slot], sems.at[slot]).wait()
        code_ref[...] = codes(carried_pattern(stack_ref, slot), row_of_ref[...], place_ref[...])
        unpack(stack_ref.at[slot], code_ref, within_ref, high_ref, low_ref, WIDE_X, half * 384)
    accumulate(step, left_high_ref, left_low_ref, high_ref, low_ref, total_ref)

    @pl.when(step == 7)
    def _():
        code_ref[...] = codes(pattern_ref[...], row_of_ref[...], place_ref[...])
        row_first = where_ref[16] * 384
        col_first = where_ref[17] * 768

        def body(i, sums):
            rows = pl.ds(pl.multiple_of(i * 48, 48), 48)
            outs = pack_rows(lambda k: total_ref[rows, k * LANES : (k + 1) * LANES], columns_ref[rows, :], 48, WIDE_S)
            for j, value in enumerate(outs):
                out_ref[rows, j * LANES : (j + 1) * LANES] = value
            entry_rows = row_first + i * 48 + lax.broadcasted_iota(jnp.int32, (48, LANES), 0)
            entry_cols = col_first + lax.broadcasted_iota(jnp.int32, (48, LANES), 1)
            for j in range(BS):
                span = slice(j * LANES, (j + 1) * LANES)
                unit = jnp.where(entry_rows == entry_cols + j * LANES, 1.0, 0.0)
                gap = jnp.where(code_ref[rows, span] >= FLAG, total_ref[rows, span] - unit, 0.0)
                sums = sums + gap * gap
            return sums

        sums = lax.fori_loop(0, 8, body, jnp.zeros((48, LANES), jnp.float32))
        defect_ref[...] = jnp.full(defect_ref.shape, jnp.sum(sums), jnp.float32)


def next_kernel(where_ref, *refs):
    blocks = refs[:16]
    patterns_ref, left_high_ref, left_low_ref, x_ref, operand_ref, product_ref, row_of_ref, place_ref, within_ref = refs[16:25]
    out_ref, stack_ref, code_ref, second_ref, high_ref, low_ref, total_ref, sems = refs[25:]
    step = pl.program_id(0)

    @pl.when(step == 0)
    def _():
        for k in range(16):
            slot = where_ref[k]
            pltpu.make_async_copy(blocks[k], stack_ref.at[slot], sems.at[slot]).start()

    for half in range(2):
        slot = 2 * step + half
        pltpu.make_async_copy(blocks[0], stack_ref.at[slot], sems.at[slot]).wait()
        code_ref[...] = codes(patterns_ref[slot], row_of_ref[...], place_ref[...])
        unpack(stack_ref.at[slot], code_ref, within_ref, high_ref, low_ref, WIDE_S, half * 384)
    accumulate(step, left_high_ref, left_low_ref, high_ref, low_ref, total_ref)

    @pl.when(step == 7)
    def _():
        code_ref[...] = codes(product_ref[...], row_of_ref[...], place_ref[...])
        second_ref[...] = codes(operand_ref[...], row_of_ref[...], place_ref[...])

        def body(i, carry):
            rows = pl.ds(pl.multiple_of(i * 48, 48), 48)
            kept = jnp.where(second_ref[rows, :] >= FLAG, x_ref[rows, :], 0.0)
            value = 1.5 * kept - 0.5 * total_ref[rows, :]
            out_ref[rows, :] = jnp.where(code_ref[rows, :] >= FLAG, value, 0.0)
            return carry

        lax.fori_loop(0, 8, body, 0)


ANY = pl.BlockSpec(memory_space=pl.ANY)


def whole(shape):
    return pl.BlockSpec(shape, lambda i, where: (0,) * len(shape))


def params():
    return pltpu.CompilerParams(vmem_limit_bytes=VMEM)


def f32(*shape):
    return jax.ShapeDtypeStruct(shape, jnp.float32)


def pack(x, pattern, row_of, until, slot, within):
    return pl.pallas_call(
        pack_kernel,
        out_shape=(f32(416, WIDE_X), f32(8, LANES)),
        scratch_shapes=[pltpu.VMEM((384, WIDE_X), jnp.int32)],
        compiler_params=params(),
        name="pack",
    )(x, pattern, row_of, until, slot, within)


def plan(pattern, row_of, until, slot, within):
    return pl.pallas_call(
        plan_kernel,
        out_shape=(jax.ShapeDtypeStruct((384, WIDE_S), jnp.int32), f32(8, LANES)),
        compiler_params=params(),
        name="plan",
    )(pattern, row_of, until, slot, within)


def left_parts(where, blocks, row_of, place, within):
    part = pl.BlockSpec((1, 384, 768), lambda i, where: (where[i], 0, 0))
    return pl.pallas_call(
        left_kernel,
        grid_spec=pltpu.PrefetchScalarGridSpec(
            num_scalar_prefetch=1,
            grid=(8,),
            in_specs=[ANY] * 8 + [whole(t.shape) for t in (row_of, place, within)],
            out_specs=[part, part],
            scratch_shapes=[
                pltpu.VMEM((8, 416, WIDE_X), jnp.float32),
                pltpu.VMEM((384, 768), jnp.float32),
                pltpu.SemaphoreType.DMA((8,)),
            ],
        ),
        out_shape=[jax.ShapeDtypeStruct((8, 384, 768), jnp.bfloat16)] * 2,
        compiler_params=params(),
        cost_estimate=pl.CostEstimate(flops=30_000_000_000, bytes_accessed=13_000_000, transcendentals=0),
        name="left_parts",
    )(where, *blocks, row_of, place, within)


def product_scratch(rows, width):
    return [pltpu.VMEM((16, rows, width), jnp.float32), pltpu.VMEM((384, 768), jnp.float32)]


def product_work():
    return [
        pltpu.VMEM((768, 768), jnp.bfloat16),
        pltpu.VMEM((768, 768), jnp.bfloat16),
        pltpu.VMEM((384, 768), jnp.float32),
        pltpu.SemaphoreType.DMA((16,)),
    ]


LEFT = pl.BlockSpec((1, 384, 768), lambda i, where: (i, 0, 0))


def square_of(where, blocks, high, low, pattern, columns, row_of, place, within):
    rest = (pattern, columns, row_of, place, within)
    return pl.pallas_call(
        square_kernel,
        grid_spec=pltpu.PrefetchScalarGridSpec(
            num_scalar_prefetch=1,
            grid=(8,),
            in_specs=[ANY] * 16 + [LEFT, LEFT] + [whole(t.shape) for t in rest],
            out_specs=[whole((384, WIDE_S)), whole((8, WIDE_S))],
            scratch_shapes=product_scratch(416, WIDE_X) + product_work(),
        ),
        out_shape=[f32(384, WIDE_S), f32(8, WIDE_S)],
        compiler_params=params(),
        cost_estimate=pl.CostEstimate(flops=30_000_000_000, bytes_accessed=20_000_000, transcendentals=0),
        name="square",
    )(where, *blocks, high, low, *rest)


def next_of(where, blocks, patterns, high, low, x, operand, product, row_of, place, within):
    rest = (x, operand, product, row_of, place, within)
    return pl.pallas_call(
        next_kernel,
        grid_spec=pltpu.PrefetchScalarGridSpec(
            num_scalar_prefetch=1,
            grid=(8,),
            in_specs=[ANY] * 16 + [whole(patterns.shape), LEFT, LEFT] + [whole(t.shape) for t in rest],
            out_specs=whole((384, 768)),
            scratch_shapes=product_scratch(384, WIDE_S) + [pltpu.VMEM((384, 768), jnp.float32)] + product_work(),
        ),
        out_shape=f32(384, 768),
        compiler_params=params(),
        cost_estimate=pl.CostEstimate(flops=30_000_000_000, bytes_accessed=20_000_000, transcendentals=0),
        name="next_iterate",
    )(where, *blocks, patterns, high, low, *rest)


def column_blocks(own):
    other = send(own, along(xh=1))
    blocks = []
    for t in (own, other):
        blocks += [t, send(t, along(z=1)), send(t, along(z=-1)), send(t, along(z=2))]
    return blocks + [send(t, along(core=1)) for t in blocks]


def column_places():
    row = lax.axis_index("row")
    xh, z, core = row // 8, row // 2 % 4, row % 2
    return [
        ((xh + a) % 2) * 8 + ((z + b) % 4) * 2 + (core + c) % 2
        for c in (0, 1)
        for a in (0, 1)
        for b in (0, 3, 1, 2)
    ]


def row_blocks(own):
    other = send(own, along(xl=1))
    blocks = []
    for t in (own, other):
        blocks += [t, send(t, along(y=1)), send(t, along(y=-1)), send(t, along(y=2))]
    return blocks


def row_places():
    col = lax.axis_index("col")
    xl, y = col // 4, col % 4
    return [((xl + a) % 2) * 4 + (y + b) % 4 for a in (0, 1) for b in (0, 3, 1, 2)]


def expand_blocks(pattern):
    rows, cols = pattern.shape
    wide = jnp.broadcast_to(pattern.astype(jnp.float32)[:, None, :, None], (rows, BS, cols, BS))
    return wide.reshape(rows * BS, cols * BS)


def matmul_high(left, right):
    return jnp.dot(left, right, precision=lax.Precision.HIGHEST, preferred_element_type=jnp.float32)


def full_rows(sign_iterate, operand_pattern, product_pattern):
    local_rows, local_cols = sign_iterate.shape
    product_mask = expand_blocks(product_pattern)
    sparse_iterate = sign_iterate * expand_blocks(operand_pattern)
    entry_rows = lax.axis_index("row") * local_rows + jnp.arange(local_rows, dtype=jnp.int32)
    entry_cols = lax.axis_index("col") * local_cols + jnp.arange(local_cols, dtype=jnp.int32)
    identity = (entry_rows[:, None] == entry_cols[None, :]).astype(jnp.float32)
    left = lax.all_gather(sparse_iterate, "col", axis=1, tiled=True)
    square = matmul_high(left, lax.all_gather(sparse_iterate, "row", axis=0, tiled=True)) * product_mask
    polynomial = 3.0 * identity - square
    sign_next = 0.5 * matmul_high(left, lax.all_gather(polynomial, "row", axis=0, tiled=True)) * product_mask
    defect = lax.psum(jnp.sum((square - identity) ** 2), AXES)
    return sign_next, defect


def per_device(sign_iterate, operand_pattern, product_pattern):
    row_of, place, until, slot_x, slot_s, within = tables()
    packed, flag_x = pack(sign_iterate, operand_pattern, row_of, until, slot_x, within)
    columns, flag_s = plan(product_pattern, row_of, until, slot_s, within)
    here = [lax.axis_index("row"), lax.axis_index("col")]
    right_where = jnp.stack(column_places() + here).astype(jnp.int32)
    left_where = jnp.stack(row_places()).astype(jnp.int32)

    patterns = lax.all_gather(product_pattern, "row", axis=0)
    left = row_blocks(packed)
    right = column_blocks(packed)
    high, low = left_parts(left_where, left, row_of, place, within)
    square, defect_tile = square_of(
        right_where, right, high, low, product_pattern, columns, row_of, place, within
    )

    part = jnp.stack([defect_tile[0, 0], jnp.maximum(flag_x[0, 0], flag_s[0, 0])])
    part = jnp.broadcast_to(part[:, None], (2, LANES))
    for step in (along(core=1), along(xh=1), along(xl=1)):
        part = part + send(part, step)
    for axis in ("z", "y"):
        part = part + send(part, along(**{axis: 2}))
        part = part + send(part, flip(axis))

    right = column_blocks(square)
    sign_next = next_of(
        right_where, right, patterns, high, low, sign_iterate, operand_pattern, product_pattern, row_of, place, within
    )
    return lax.cond(
        part[1, 0] > 0.0,
        lambda: full_rows(sign_iterate, operand_pattern, product_pattern),
        lambda: (sign_next, part[0, 0]),
    )


def flip(axis):
    if axis == "z":
        return lambda a, b, c, d, e: (a, b ^ 1, c, d, e)
    return lambda a, b, c, d, e: (a, b, c, d, e ^ 1)


def solution(mesh):
    spec = P("row", "col")
    return jax.shard_map(
        per_device, mesh=mesh, in_specs=(spec, spec, spec), out_specs=(spec, P()), check_vma=False
    )
```

time: 448 us -> 381 us (0.85)
  Pallas kernels: 0 us -> 189 us
  waiting for transfers between devices: 212 us -> 73.8 us
  blocking collectives: 102 us -> 24 us
  starting transfers between devices: 0.3 us -> 66.5 us
  matrix products: 57.2 us -> 0 us
  local copies, waits for them, and re-layouts: 60.5 us -> 9.38 us
    all_gather x3 -> x0, waiting for transfers between devices: 211 us -> none  [the longest x2 138 us: product(): column_block = lax.all_gather(right_part, 'row', axis=0, tiled=True)]
    pallas_call x0 -> x5, Pallas kernels: none -> 189 us  [the longest x1 82 us: next_of(): pl.pallas_call(next_kernel, grid_spec=pltpu.PrefetchScalarGridSpec(num_sc...]
    psum x1 -> x0, blocking collectives: 102 us -> none  [per_device(): defect = lax.psum(local_defect, ('row', 'col'))]
    ppermute x0 -> x44, waiting for transfers between devices: none -> 73.8 us  [send(): return lax.ppermute(value, AXES, pairs)]
    ppermute x0 -> x44, starting transfers between devices: none -> 66.5 us  [send(): return lax.ppermute(value, AXES, pairs)]
    dot_general x2 -> x0, matrix products: 57.2 us -> none  [matmul_high(): jnp.dot(left, right, precision=lax.Precision.HIGHEST, preferred_element_t...]
    reshape x2 -> x0, local copies, waits for them, and re-layouts: 37 us -> none  [expand_blocks(): return wide.reshape(count_rows * BS, count_cols * BS)]
    all_gather x0 -> x1, blocking collectives: none -> 24 us  [per_device(): patterns = lax.all_gather(product_pattern, 'row', axis=0)]
  transfers between devices with their start and end apart: 3 -> 44, of which waited for: 3 -> 18; matrix products, arithmetic and copies ran while one was open for 7% -> 1% of each run, Pallas kernels for 0% -> 7%
where the time goes in v1:
time: 381 us
  Pallas kernels  189 us (50%)
  waiting for transfers between devices  73.8 us (19%)
  starting transfers between devices  66.5 us (17%)
  blocking collectives  24 us (6%)
  between operations  16.6 us (4%)
  local copies, waits for them, and re-layouts  9.38 us (2%)
    pallas_call x1, Pallas kernels, next_of(): pl.pallas_call(next_kernel, grid_spec=pltpu.PrefetchScalarGridSpec(num_sc...  82 us
    pallas_call x1, Pallas kernels, square_of(): pl.pallas_call(square_kernel, grid_spec=pltpu.PrefetchScalarGridSpec(num_...  75.2 us
    ppermute x44, waiting for transfers between devices, send(): return lax.ppermute(value, AXES, pairs)  73.8 us
    ppermute x44, starting transfers between devices, send(): return lax.ppermute(value, AXES, pairs)  66.5 us
    pallas_call x1, Pallas kernels, left_parts(): pl.pallas_call(left_kernel, grid_spec=pltpu.PrefetchScalarGridSpec(num_sc...  24.4 us
    all_gather x1, blocking collectives, per_device(): patterns = lax.all_gather(product_pattern, 'row', axis=0)  24 us
  transfers between devices with their start and end apart: 44, of which 18 were waited for; matrix products, arithmetic and copies ran while one was open for 1% of the time, Pallas kernels for 7%

profile of v1, /device:TPU:1, one launch (start us, length us, event | category | flops | bytes accessed | tf_op | source)
XLA Modules:
  0.0 380.7 jit_solution(9852667719870622425)
XLA Ops:
  7.2 5.1 %pack.1 = (f32[416,256]{1,0:T(8,128)}, f32[8,128]{1,0:T(8,128)}) custom-call(f32[384,768]{1,0:T(8,128)} %refs_19_.1, s32[64,128]{1,0:T(8,128)} %refs_20_.2, bf16[384,64]{1,0:T(8,128)(2,1)} %constant.259.clone.row_of_ref.refs_8_.refs_20_.refs_22_, bf16[128,128]{1,0:T(8,128)(2,1)} %constant.261.clone.until_ref, bf16[128,256]{1,0:T(8,128)(2,1)} %constant.262.clone.slot_ref, ...), custom_call_target="tpu_custom_call" | custom-call | tf_op jit(solution)/shard_map/pack/pallas_call | solution.py:264
  12.3 2.0 collective-permute-start.18
  14.3 2.9 collective-permute-start.17
  18.7 1.8 collective-permute-start.7
  20.5 3.1 collective-permute-done.18.refs_4_
  23.5 3.2 collective-permute-start.3
  26.7 3.6 collective-permute-start.2
  30.3 6.0 %collective-permute-done.16.refs_2_ = f32[416,256]{1,0:T(8,128)S(1)} collective-permute-done((f32[416,256]{1,0:T(8,128)}, f32[416,256]{1,0:T(8,128)S(1)}, u32[]{:S(2)}, u32[]{:S(2)}) %collective-permute-start.16) | collective-permute-done | bytes 426016 | tf_op jit(solution)/shard_map/ppermute | solution.py:30
  36.3 3.8 collective-permute-start.1
  40.1 1.6 collective-permute-start.21
  41.7 2.7 collective-permute-start.20
  44.5 5.6 %collective-permute-done.1.refs_2_ = f32[416,256]{1,0:T(8,128)S(1)} collective-permute-done((f32[416,256]{1,0:T(8,128)}, f32[416,256]{1,0:T(8,128)S(1)}, u32[]{:S(2)}, u32[]{:S(2)}) %collective-permute-start.1) | collective-permute-done | bytes 426016 | tf_op jit(solution)/shard_map/ppermute | solution.py:30
  50.0 1.4 collective-permute-start.11
  52.4 2.5 collective-permute-start.5
  54.8 7.6 %collective-permute-done.20.refs_6_ = f32[416,256]{1,0:T(8,128)S(1)} collective-permute-done((f32[416,256]{1,0:T(8,128)S(1)}, f32[416,256]{1,0:T(8,128)S(1)}, u32[]{:S(2)}, u32[]{:S(2)}) %collective-permute-start.20) | collective-permute-done | bytes 426016 | tf_op jit(solution)/shard_map/ppermute | solution.py:30
  62.7 1.4 collective-permute-start.10
  64.4 1.2 slice.16
  65.6 2.8 plan.1
  68.4 1.2 slice.17
  72.9 1.6 collective-permute-done.5.refs_6_
  76.0 24.4 %left_parts.1 = (bf16[8,384,768]{2,1,0:T(8,128)(2,1)}, bf16[8,384,768]{2,1,0:T(8,128)(2,1)}) custom-call(s32[8]{0:T(128)} %stack.117.where_ref, f32[416,256]{1,0:T(8,128)} %get-tuple-element.25.refs_0_, f32[416,256]{1,0:T(8,128)} %copy-done.25, f32[416,256]{1,0:T(8,128)} %copy-done.24, f32[416,256]{1,0:T(8,128)} %copy-done.22, f32[416,256]{1,0:T(8,128)} %copy-done.21, ...), custom_call_target="tpu_custom_call" | custom-call | flops 30000001024 | bytes 13000000 | tf_op jit(solution)/shard_map/left_parts/pallas_call | solution.py:284
  101.8 75.2 %square.1 = (f32[384,384]{1,0:T(8,128)}, f32[8,384]{1,0:T(8,128)}) custom-call(s32[18]{0:T(128)} %stack.108.where_ref, f32[416,256]{1,0:T(8,128)} %get-tuple-element.25.refs_0_, f32[416,256]{1,0:T(8,128)} %copy-done.26, f32[416,256]{1,0:T(8,128)} %copy-done.23, f32[416,256]{1,0:T(8,128)} %copy-done.20, f32[416,256]{1,0:T(8,128)} %copy-done.19, ...), custom_call_target="tpu_custom_call" | custom-call | flops 30000001024 | bytes 20000000 | tf_op jit(solution)/shard_map/square/pallas_call | solution.py:322
  177.0 1.2 slice.15
  179.0 1.1 collective-permute-done.22
  180.2 3.0 collective-permute-start.23
  183.2 1.0 collective-permute-done.23
  184.5 2.2 collective-permute-done.24
  186.6 2.0 collective-permute-start.25
  188.7 1.9 collective-permute-done.25
  190.6 2.7 collective-permute-done.26
  193.3 2.8 collective-permute-start.27
  196.1 1.1 collective-permute-done.27
  197.2 2.1 collective-permute-start.28
  199.3 2.9 collective-permute-start.32
  202.3 6.2 %collective-permute-start.36 = (f32[384,384]{1,0:T(8,128)}, f32[384,384]{1,0:T(8,128)S(1)}, u32[]{:S(2)}, u32[]{:S(2)}) collective-permute-start(f32[384,384]{1,0:T(8,128)} %get-tuple-element.32.refs_0_), channel_id=1, source_target_pairs={{0,8},{1,9},{2,10},{3,11},{4,12},{5,13},{6,14},{7,15},{8,0},{9,1},... | collective-permute-start | bytes 1769480 | tf_op jit(solution)/shard_map/ppermute | solution.py:30
  208.5 1.1 collective-permute-start.31
  209.5 1.1 collective-permute-start.30
  211.0 5.8 %collective-permute-start.40 = (f32[384,384]{1,0:T(8,128)S(1)}, f32[384,384]{1,0:T(8,128)S(1)}, u32[]{:S(2)}, u32[]{:S(2)}) collective-permute-start(f32[384,384]{1,0:T(8,128)S(1)} %collective-permute-done.32.refs_4_), channel_id=1, source_target_pairs={{0,8},{1,9},{2,10},{3,11},{4,12},{5,13},{6,14},{7,15},{8,0},{9,1},... | collective-permute-start | bytes 1769480 | tf_op jit(solution)/shard_map/ppermute | solution.py:30
  216.8 1.3 collective-permute-start.35
  218.2 7.0 %collective-permute-done.31.refs_3_ = f32[384,384]{1,0:T(8,128)S(1)} collective-permute-done((f32[384,384]{1,0:T(8,128)}, f32[384,384]{1,0:T(8,128)S(1)}, u32[]{:S(2)}, u32[]{:S(2)}) %collective-permute-start.31) | collective-permute-done | bytes 589856 | tf_op jit(solution)/shard_map/ppermute | solution.py:30
  225.2 1.6 collective-permute-start.34
  226.8 10.2 %collective-permute-done.30.refs_2_ = f32[384,384]{1,0:T(8,128)S(1)} collective-permute-done((f32[384,384]{1,0:T(8,128)}, f32[384,384]{1,0:T(8,128)S(1)}, u32[]{:S(2)}, u32[]{:S(2)}) %collective-permute-start.30) | collective-permute-done | bytes 589856 | tf_op jit(solution)/shard_map/ppermute | solution.py:30
  237.0 1.0 collective-permute-start.33
  239.1 11.4 %collective-permute-done.35.refs_7_ = f32[384,384]{1,0:T(8,128)S(1)} collective-permute-done((f32[384,384]{1,0:T(8,128)S(1)}, f32[384,384]{1,0:T(8,128)S(1)}, u32[]{:S(2)}, u32[]{:S(2)}) %collective-permute-start.35) | collective-permute-done | bytes 589856 | tf_op jit(solution)/shard_map/ppermute | solution.py:30
  250.5 1.2 collective-permute-start.37
  251.7 10.7 %collective-permute-done.34.refs_6_ = f32[384,384]{1,0:T(8,128)S(1)} collective-permute-done((f32[384,384]{1,0:T(8,128)S(1)}, f32[384,384]{1,0:T(8,128)S(1)}, u32[]{:S(2)}, u32[]{:S(2)}) %collective-permute-start.34) | collective-permute-done | bytes 589856 | tf_op jit(solution)/shard_map/ppermute | solution.py:30
  264.0 24.0 %all-gather = s32[1024,128]{1,0:T(8,128)} all-gather(s32[64,128]{1,0:T(8,128)S(1)} %copy-done.1), channel_id=2, replica_groups=mesh['row'=16,'col'=8] {'row'}, dimensions={0}, use_global_device_ids=true | all-gather | bytes 557056 | tf_op jit(solution)/shard_map/all_gather | solution.py:422
  291.3 82.0 %next_iterate.1 = f32[384,768]{1,0:T(8,128)} custom-call(s32[18]{0:T(128)} %stack.108.where_ref, f32[384,384]{1,0:T(8,128)} %get-tuple-element.32.refs_0_, f32[384,384]{1,0:T(8,128)} %copy-done.7, f32[384,384]{1,0:T(8,128)} %copy-done.6, f32[384,384]{1,0:T(8,128)} %copy-done.5, f32[384,384]{1,0:T(8,128)} %copy-done.3, f32[384,384]{1,0:T(8,128)} %copy-done.11, ...), custom_call_target="tpu_custom_call" | custom-call | flops 30000001024 | bytes 20000000 | tf_op jit(solution)/shard_map/next_iterate/pallas_call | solution.py:340
  (133 shorter events, 15.3 us)
Async XLA Ops:
  12.3 11.3 %collective-permute-start.18 = (f32[416,256]{1,0:T(8,128)}, f32[416,256]{1,0:T(8,128)S(1)}, u32[]{:S(2)}, u32[]{:S(2)}) collective-permute-start(f32[416,256]{1,0:T(8,128)} %get-tuple-element.25.refs_0_), channel_id=1, source_target_pairs={{0,4},{1,5},{2,6},{3,7},{4,0},{5,1},{6,2},{7,3},{8,12},{9,13},{10,... | collective-permute-start | bytes 1277960 | tf_op jit(solution)/shard_map/ppermute | solution.py:30
  14.3 12.4 %collective-permute-start.17 = (f32[416,256]{1,0:T(8,128)}, f32[416,256]{1,0:T(8,128)S(1)}, u32[]{:S(2)}, u32[]{:S(2)}) collective-permute-start(f32[416,256]{1,0:T(8,128)} %get-tuple-element.25.refs_0_), channel_id=1, source_target_pairs={{0,2},{1,3},{2,0},{3,1},{4,6},{5,7},{6,4},{7,5},{8,10},{9,11},{10,... | collective-permute-start | bytes 1277960 | tf_op jit(solution)/shard_map/ppermute | solution.py:30
  17.2 19.1 %collective-permute-start.16 = (f32[416,256]{1,0:T(8,128)}, f32[416,256]{1,0:T(8,128)S(1)}, u32[]{:S(2)}, u32[]{:S(2)}) collective-permute-start(f32[416,256]{1,0:T(8,128)} %get-tuple-element.25.refs_0_), channel_id=1, source_target_pairs={{0,3},{1,0},{2,1},{3,2},{4,7},{5,4},{6,5},{7,6},{8,11},{9,8},{10,9... | collective-permute-start | bytes 1277960 | tf_op jit(solution)/shard_map/ppermute | solution.py:30
  18.0 22.1 %collective-permute-start.15 = (f32[416,256]{1,0:T(8,128)}, f32[416,256]{1,0:T(8,128)S(1)}, u32[]{:S(2)}, u32[]{:S(2)}) collective-permute-start(f32[416,256]{1,0:T(8,128)} %get-tuple-element.25.refs_0_), channel_id=1, source_target_pairs={{0,1},{1,2},{2,3},{3,0},{4,5},{5,6},{6,7},{7,4},{8,9},{9,10},{10,1... | collective-permute-start | bytes 1277960 | tf_op jit(solution)/shard_map/ppermute | solution.py:30
  18.7 21.4 %collective-permute-start.7 = (f32[416,256]{1,0:T(8,128)}, f32[416,256]{1,0:T(8,128)S(1)}, u32[]{:S(2)}, u32[]{:S(2)}) collective-permute-start(f32[416,256]{1,0:T(8,128)} %get-tuple-element.25.refs_0_), channel_id=1, source_target_pairs={{0,8},{1,9},{2,10},{3,11},{4,12},{5,13},{6,14},{7,15},{8,0},{9,1},... | collective-permute-start | bytes 1277960 | tf_op jit(solution)/shard_map/ppermute | solution.py:30
  23.5 18.2 %collective-permute-start.3 = (f32[416,256]{1,0:T(8,128)}, f32[416,256]{1,0:T(8,128)S(1)}, u32[]{:S(2)}, u32[]{:S(2)}) collective-permute-start(f32[416,256]{1,0:T(8,128)} %get-tuple-element.25.refs_0_), channel_id=1, source_target_pairs={{0,64},{1,65},{2,66},{3,67},{4,68},{5,69},{6,70},{7,71},{8,72},{9,... | collective-permute-start | bytes 1277960 | tf_op jit(solution)/shard_map/ppermute | solution.py:30
  26.7 17.7 %collective-permute-start.2 = (f32[416,256]{1,0:T(8,128)}, f32[416,256]{1,0:T(8,128)S(1)}, u32[]{:S(2)}, u32[]{:S(2)}) collective-permute-start(f32[416,256]{1,0:T(8,128)} %get-tuple-element.25.refs_0_), channel_id=1, source_target_pairs={{0,32},{1,33},{2,34},{3,35},{4,36},{5,37},{6,38},{7,39},{8,40},{9,... | collective-permute-start | bytes 1277960 | tf_op jit(solution)/shard_map/ppermute | solution.py:30
  36.3 13.7 %collective-permute-start.1 = (f32[416,256]{1,0:T(8,128)}, f32[416,256]{1,0:T(8,128)S(1)}, u32[]{:S(2)}, u32[]{:S(2)}) collective-permute-start(f32[416,256]{1,0:T(8,128)} %get-tuple-element.25.refs_0_), channel_id=1, source_target_pairs={{0,48},{1,49},{2,50},{3,51},{4,52},{5,53},{6,54},{7,55},{8,56},{9,... | collective-permute-start | bytes 1277960 | tf_op jit(solution)/shard_map/ppermute | solution.py:30
  40.1 11.4 %collective-permute-start = (f32[416,256]{1,0:T(8,128)}, f32[416,256]{1,0:T(8,128)S(1)}, u32[]{:S(2)}, u32[]{:S(2)}) collective-permute-start(f32[416,256]{1,0:T(8,128)} %get-tuple-element.25.refs_0_), channel_id=1, source_target_pairs={{0,16},{1,17},{2,18},{3,19},{4,20},{5,21},{6,22},{7,23},{8,24},{9,... | collective-permute-start | bytes 1277960 | tf_op jit(solution)/shard_map/ppermute | solution.py:30
  40.1 12.3 %collective-permute-start.21 = (f32[416,256]{1,0:T(8,128)S(1)}, f32[416,256]{1,0:T(8,128)S(1)}, u32[]{:S(2)}, u32[]{:S(2)}) collective-permute-start(f32[416,256]{1,0:T(8,128)S(1)} %collective-permute-done.18.refs_4_), channel_id=1, source_target_pairs={{0,2},{1,3},{2,0},{3,1},{4,6},{5,7},{6,4},{7,5},{8,10},{9,11},{10,... | collective-permute-start | bytes 1277960 | tf_op jit(solution)/shard_map/ppermute | solution.py:30
  41.7 20.7 %collective-permute-start.20 = (f32[416,256]{1,0:T(8,128)S(1)}, f32[416,256]{1,0:T(8,128)S(1)}, u32[]{:S(2)}, u32[]{:S(2)}) collective-permute-start(f32[416,256]{1,0:T(8,128)S(1)} %collective-permute-done.18.refs_4_), channel_id=1, source_target_pairs={{0,3},{1,0},{2,1},{3,2},{4,7},{5,4},{6,5},{7,6},{8,11},{9,8},{10,9... | collective-permute-start | bytes 1277960 | tf_op jit(solution)/shard_map/ppermute | solution.py:30
  44.4 18.2 %collective-permute-start.19 = (f32[416,256]{1,0:T(8,128)S(1)}, f32[416,256]{1,0:T(8,128)S(1)}, u32[]{:S(2)}, u32[]{:S(2)}) collective-permute-start(f32[416,256]{1,0:T(8,128)S(1)} %collective-permute-done.18.refs_4_), channel_id=1, source_target_pairs={{0,1},{1,2},{2,3},{3,0},{4,5},{5,6},{6,7},{7,4},{8,9},{9,10},{10,1... | collective-permute-start | bytes 1277960 | tf_op jit(solution)/shard_map/ppermute | solution.py:30
  50.0 22.2 %collective-permute-start.11 = (f32[416,256]{1,0:T(8,128)S(1)}, f32[416,256]{1,0:T(8,128)}, u32[]{:S(2)}, u32[]{:S(2)}) collective-permute-start(f32[416,256]{1,0:T(8,128)S(1)} %collective-permute-done.3.refs_4_), channel_id=1, source_target_pairs={{0,8},{1,9},{2,10},{3,11},{4,12},{5,13},{6,14},{7,15},{8,0},{9,1},... | collective-permute-start | bytes 1277960 | tf_op jit(solution)/shard_map/ppermute | solution.py:30
  51.4 21.4 %collective-permute-start.6 = (f32[416,256]{1,0:T(8,128)S(1)}, f32[416,256]{1,0:T(8,128)}, u32[]{:S(2)}, u32[]{:S(2)}) collective-permute-start(f32[416,256]{1,0:T(8,128)S(1)} %collective-permute-done.3.refs_4_), channel_id=1, source_target_pairs={{0,32},{1,33},{2,34},{3,35},{4,36},{5,37},{6,38},{7,39},{8,40},{9,... | collective-permute-start | bytes 1277960 | tf_op jit(solution)/shard_map/ppermute | solution.py:30
  52.4 22.1 %collective-permute-start.5 = (f32[416,256]{1,0:T(8,128)S(1)}, f32[416,256]{1,0:T(8,128)}, u32[]{:S(2)}, u32[]{:S(2)}) collective-permute-start(f32[416,256]{1,0:T(8,128)S(1)} %collective-permute-done.3.refs_4_), channel_id=1, source_target_pairs={{0,48},{1,49},{2,50},{3,51},{4,52},{5,53},{6,54},{7,55},{8,56},{9,... | collective-permute-start | bytes 1277960 | tf_op jit(solution)/shard_map/ppermute | solution.py:30
  62.4 12.9 %collective-permute-start.4 = (f32[416,256]{1,0:T(8,128)S(1)}, f32[416,256]{1,0:T(8,128)}, u32[]{:S(2)}, u32[]{:S(2)}) collective-permute-start(f32[416,256]{1,0:T(8,128)S(1)} %collective-permute-done.3.refs_4_), channel_id=1, source_target_pairs={{0,16},{1,17},{2,18},{3,19},{4,20},{5,21},{6,22},{7,23},{8,24},{9,... | collective-permute-start | bytes 1277960 | tf_op jit(solution)/shard_map/ppermute | solution.py:30
  62.7 13.3 %collective-permute-start.10 = (f32[416,256]{1,0:T(8,128)S(1)}, f32[416,256]{1,0:T(8,128)}, u32[]{:S(2)}, u32[]{:S(2)}) collective-permute-start(f32[416,256]{1,0:T(8,128)S(1)} %collective-permute-done.2.refs_3_), channel_id=1, source_target_pairs={{0,8},{1,9},{2,10},{3,11},{4,12},{5,13},{6,14},{7,15},{8,0},{9,1},... | collective-permute-start | bytes 1277960 | tf_op jit(solution)/shard_map/ppermute | solution.py:30
  72.2 28.2 %collective-permute-start.9 = (f32[416,256]{1,0:T(8,128)S(1)}, f32[416,256]{1,0:T(8,128)S(1)}, u32[]{:S(2)}, u32[]{:S(2)}) collective-permute-start(f32[416,256]{1,0:T(8,128)S(1)} %collective-permute-done.1.refs_2_), channel_id=1, source_target_pairs={{0,8},{1,9},{2,10},{3,11},{4,12},{5,13},{6,14},{7,15},{8,0},{9,1},... | collective-permute-start | bytes 1277960 | tf_op jit(solution)/shard_map/ppermute | solution.py:30
  72.8 27.7 %collective-permute-start.8 = (f32[416,256]{1,0:T(8,128)}, f32[416,256]{1,0:T(8,128)S(1)}, u32[]{:S(2)}, u32[]{:S(2)}) collective-permute-start(f32[416,256]{1,0:T(8,128)} %copy-done.26), channel_id=1, source_target_pairs={{0,8},{1,9},{2,10},{3,11},{4,12},{5,13},{6,14},{7,15},{8,0},{9,1},... | collective-permute-start | bytes 1277960 | tf_op jit(solution)/shard_map/ppermute | solution.py:30
  74.5 26.0 %collective-permute-start.14 = (f32[416,256]{1,0:T(8,128)}, f32[416,256]{1,0:T(8,128)S(1)}, u32[]{:S(2)}, u32[]{:S(2)}) collective-permute-start(f32[416,256]{1,0:T(8,128)} %collective-permute-done.6.refs_7_), channel_id=1, source_target_pairs={{0,8},{1,9},{2,10},{3,11},{4,12},{5,13},{6,14},{7,15},{8,0},{9,1},... | collective-permute-start | bytes 1277960 | tf_op jit(solution)/shard_map/ppermute | solution.py:30
  75.4 25.1 %collective-permute-start.13 = (f32[416,256]{1,0:T(8,128)}, f32[416,256]{1,0:T(8,128)S(1)}, u32[]{:S(2)}, u32[]{:S(2)}) collective-permute-start(f32[416,256]{1,0:T(8,128)} %collective-permute-done.5.refs_6_), channel_id=1, source_target_pairs={{0,8},{1,9},{2,10},{3,11},{4,12},{5,13},{6,14},{7,15},{8,0},{9,1},... | collective-permute-start | bytes 1277960 | tf_op jit(solution)/shard_map/ppermute | solution.py:30
  76.0 24.5 %collective-permute-start.12 = (f32[416,256]{1,0:T(8,128)}, f32[416,256]{1,0:T(8,128)S(1)}, u32[]{:S(2)}, u32[]{:S(2)}) collective-permute-start(f32[416,256]{1,0:T(8,128)} %collective-permute-done.4.refs_5_), channel_id=1, source_target_pairs={{0,8},{1,9},{2,10},{3,11},{4,12},{5,13},{6,14},{7,15},{8,0},{9,1},... | collective-permute-start | bytes 1277960 | tf_op jit(solution)/shard_map/ppermute | solution.py:30
  101.8 189.5 %copy-start = (f32[384,768]{1,0:T(8,128)S(1)}, f32[384,768]{1,0:T(8,128)}, u32[]{:S(2)}) copy-start(f32[384,768]{1,0:T(8,128)} %refs_19_.1) | copy-start | bytes 3538948
  101.8 189.6 %copy-start.2 = (s32[64,128]{1,0:T(8,128)S(1)}, s32[64,128]{1,0:T(8,128)}, u32[]{:S(2)}) copy-start(s32[64,128]{1,0:T(8,128)} %refs_20_.2) | copy-start | bytes 98308
  179.0 1.1 collective-permute-start.22
  180.2 3.9 %collective-permute-start.23 = (f32[2,128]{1,0:T(2,128)S(1)}, f32[2,128]{1,0:T(2,128)S(1)}, u32[]{:S(2)}, u32[]{:S(2)}) collective-permute-start(f32[2,128]{1,0:T(2,128)S(1)} %broadcast_add_fusion), channel_id=1, source_target_pairs={{0,64},{1,65},{2,66},{3,67},{4,68},{5,69},{6,70},{7,71},{8,72},{9,... | collective-permute-start | bytes 3080 | tf_op jit(solution)/shard_map/ppermute | solution.py:30
  184.2 2.4 collective-permute-start.24
  186.6 3.9 %collective-permute-start.25 = (f32[2,128]{1,0:T(2,128)S(1)}, f32[2,128]{1,0:T(2,128)S(1)}, u32[]{:S(2)}, u32[]{:S(2)}) collective-permute-start(f32[2,128]{1,0:T(2,128)S(1)} %add.368), channel_id=1, source_target_pairs={{0,32},{1,33},{2,34},{3,35},{4,36},{5,37},{6,38},{7,39},{8,40},{9,... | collective-permute-start | bytes 3080 | tf_op jit(solution)/shard_map/ppermute | solution.py:30
  190.6 2.7 collective-permute-start.26
  193.3 3.9 %collective-permute-start.27 = (f32[2,128]{1,0:T(2,128)S(1)}, f32[2,128]{1,0:T(2,128)S(1)}, u32[]{:S(2)}, u32[]{:S(2)}) collective-permute-start(f32[2,128]{1,0:T(2,128)S(1)} %add.370), channel_id=1, source_target_pairs={{0,2},{1,3},{2,0},{3,1},{4,6},{5,7},{6,4},{7,5},{8,10},{9,11},{10,... | collective-permute-start | bytes 3080 | tf_op jit(solution)/shard_map/ppermute | solution.py:30
  197.2 13.4 %collective-permute-start.28 = (f32[2,128]{1,0:T(2,128)S(1)}, f32[2,128]{1,0:T(2,128)S(1)}, u32[]{:S(2)}, u32[]{:S(2)}) collective-permute-start(f32[2,128]{1,0:T(2,128)S(1)} %add.371), channel_id=1, source_target_pairs={{0,1},{1,0},{2,3},{3,2},{4,5},{5,4},{6,7},{7,6},{8,9},{9,8},{10,11... | collective-permute-start | bytes 3080 | tf_op jit(solution)/shard_map/ppermute | solution.py:30
  199.3 11.7 %collective-permute-start.32 = (f32[384,384]{1,0:T(8,128)}, f32[384,384]{1,0:T(8,128)S(1)}, u32[]{:S(2)}, u32[]{:S(2)}) collective-permute-start(f32[384,384]{1,0:T(8,128)} %get-tuple-element.32.refs_0_), channel_id=1, source_target_pairs={{0,64},{1,65},{2,66},{3,67},{4,68},{5,69},{6,70},{7,71},{8,72},{9,... | collective-permute-start | bytes 1769480 | tf_op jit(solution)/shard_map/ppermute | solution.py:30
  202.3 14.6 %collective-permute-start.36 = (f32[384,384]{1,0:T(8,128)}, f32[384,384]{1,0:T(8,128)S(1)}, u32[]{:S(2)}, u32[]{:S(2)}) collective-permute-start(f32[384,384]{1,0:T(8,128)} %get-tuple-element.32.refs_0_), channel_id=1, source_target_pairs={{0,8},{1,9},{2,10},{3,11},{4,12},{5,13},{6,14},{7,15},{8,0},{9,1},... | collective-permute-start | bytes 1769480 | tf_op jit(solution)/shard_map/ppermute | solution.py:30
  208.5 16.7 %collective-permute-start.31 = (f32[384,384]{1,0:T(8,128)}, f32[384,384]{1,0:T(8,128)S(1)}, u32[]{:S(2)}, u32[]{:S(2)}) collective-permute-start(f32[384,384]{1,0:T(8,128)} %get-tuple-element.32.refs_0_), channel_id=1, source_target_pairs={{0,32},{1,33},{2,34},{3,35},{4,36},{5,37},{6,38},{7,39},{8,40},{9,... | collective-permute-start | bytes 1769480 | tf_op jit(solution)/shard_map/ppermute | solution.py:30
  209.5 27.5 %collective-permute-start.30 = (f32[384,384]{1,0:T(8,128)}, f32[384,384]{1,0:T(8,128)S(1)}, u32[]{:S(2)}, u32[]{:S(2)}) collective-permute-start(f32[384,384]{1,0:T(8,128)} %get-tuple-element.32.refs_0_), channel_id=1, source_target_pairs={{0,48},{1,49},{2,50},{3,51},{4,52},{5,53},{6,54},{7,55},{8,56},{9,... | collective-permute-start | bytes 1769480 | tf_op jit(solution)/shard_map/ppermute | solution.py:30
  210.6 27.7 %collective-permute-start.29 = (f32[384,384]{1,0:T(8,128)}, f32[384,384]{1,0:T(8,128)S(1)}, u32[]{:S(2)}, u32[]{:S(2)}) collective-permute-start(f32[384,384]{1,0:T(8,128)} %get-tuple-element.32.refs_0_), channel_id=1, source_target_pairs={{0,16},{1,17},{2,18},{3,19},{4,20},{5,21},{6,22},{7,23},{8,24},{9,... | collective-permute-start | bytes 1769480 | tf_op jit(solution)/shard_map/ppermute | solution.py:30
  211.0 80.3 %copy-start.3 = (f32[384,384]{1,0:T(8,128)}, f32[384,384]{1,0:T(8,128)S(1)}, u32[]{:S(2)}) copy-start(f32[384,384]{1,0:T(8,128)S(1)} %collective-permute-done.32.refs_4_) | copy-start | bytes 1769476
  211.0 28.0 %collective-permute-start.40 = (f32[384,384]{1,0:T(8,128)S(1)}, f32[384,384]{1,0:T(8,128)S(1)}, u32[]{:S(2)}, u32[]{:S(2)}) collective-permute-start(f32[384,384]{1,0:T(8,128)S(1)} %collective-permute-done.32.refs_4_), channel_id=1, source_target_pairs={{0,8},{1,9},{2,10},{3,11},{4,12},{5,13},{6,14},{7,15},{8,0},{9,1},... | collective-permute-start | bytes 1769480 | tf_op jit(solution)/shard_map/ppermute | solution.py:30
  216.8 74.4 %copy-start.4 = (f32[384,384]{1,0:T(8,128)}, f32[384,384]{1,0:T(8,128)S(1)}, u32[]{:S(2)}) copy-start(f32[384,384]{1,0:T(8,128)S(1)} %collective-permute-done.36.refs_8_) | copy-start | bytes 1769476
  216.8 33.7 %collective-permute-start.35 = (f32[384,384]{1,0:T(8,128)S(1)}, f32[384,384]{1,0:T(8,128)S(1)}, u32[]{:S(2)}, u32[]{:S(2)}) collective-permute-start(f32[384,384]{1,0:T(8,128)S(1)} %collective-permute-done.32.refs_4_), channel_id=1, source_target_pairs={{0,32},{1,33},{2,34},{3,35},{4,36},{5,37},{6,38},{7,39},{8,40},{9,... | collective-permute-start | bytes 1769480 | tf_op jit(solution)/shard_map/ppermute | solution.py:30
  225.2 37.2 %collective-permute-start.34 = (f32[384,384]{1,0:T(8,128)S(1)}, f32[384,384]{1,0:T(8,128)S(1)}, u32[]{:S(2)}, u32[]{:S(2)}) collective-permute-start(f32[384,384]{1,0:T(8,128)S(1)} %collective-permute-done.32.refs_4_), channel_id=1, source_target_pairs={{0,48},{1,49},{2,50},{3,51},{4,52},{5,53},{6,54},{7,55},{8,56},{9,... | collective-permute-start | bytes 1769480 | tf_op jit(solution)/shard_map/ppermute | solution.py:30
  237.0 26.3 %collective-permute-start.33 = (f32[384,384]{1,0:T(8,128)S(1)}, f32[384,384]{1,0:T(8,128)S(1)}, u32[]{:S(2)}, u32[]{:S(2)}) collective-permute-start(f32[384,384]{1,0:T(8,128)S(1)} %collective-permute-done.32.refs_4_), channel_id=1, source_target_pairs={{0,16},{1,17},{2,18},{3,19},{4,20},{5,21},{6,22},{7,23},{8,24},{9,... | collective-permute-start | bytes 1769480 | tf_op jit(solution)/shard_map/ppermute | solution.py:30
  238.3 25.6 %collective-permute-start.39 = (f32[384,384]{1,0:T(8,128)S(1)}, f32[384,384]{1,0:T(8,128)S(1)}, u32[]{:S(2)}, u32[]{:S(2)}) collective-permute-start(f32[384,384]{1,0:T(8,128)S(1)} %collective-permute-done.31.refs_3_), channel_id=1, source_target_pairs={{0,8},{1,9},{2,10},{3,11},{4,12},{5,13},{6,14},{7,15},{8,0},{9,1},... | collective-permute-start | bytes 1769480 | tf_op jit(solution)/shard_map/ppermute | solution.py:30
  239.0 50.1 %collective-permute-start.38 = (f32[384,384]{1,0:T(8,128)S(1)}, f32[384,384]{1,0:T(8,128)S(1)}, u32[]{:S(2)}, u32[]{:S(2)}) collective-permute-start(f32[384,384]{1,0:T(8,128)S(1)} %collective-permute-done.30.refs_2_), channel_id=1, source_target_pairs={{0,8},{1,9},{2,10},{3,11},{4,12},{5,13},{6,14},{7,15},{8,0},{9,1},... | collective-permute-start | bytes 1769480 | tf_op jit(solution)/shard_map/ppermute | solution.py:30
  250.5 38.7 %collective-permute-start.37 = (f32[384,384]{1,0:T(8,128)S(1)}, f32[384,384]{1,0:T(8,128)S(1)}, u32[]{:S(2)}, u32[]{:S(2)}) collective-permute-start(f32[384,384]{1,0:T(8,128)S(1)} %collective-permute-done.29.refs_1_), channel_id=1, source_target_pairs={{0,8},{1,9},{2,10},{3,11},{4,12},{5,13},{6,14},{7,15},{8,0},{9,1},... | collective-permute-start | bytes 1769480 | tf_op jit(solution)/shard_map/ppermute | solution.py:30
  262.4 26.8 %collective-permute-start.43 = (f32[384,384]{1,0:T(8,128)S(1)}, f32[384,384]{1,0:T(8,128)S(1)}, u32[]{:S(2)}, u32[]{:S(2)}) collective-permute-start(f32[384,384]{1,0:T(8,128)S(1)} %collective-permute-done.35.refs_7_), channel_id=1, source_target_pairs={{0,8},{1,9},{2,10},{3,11},{4,12},{5,13},{6,14},{7,15},{8,0},{9,1},... | collective-permute-start | bytes 1769480 | tf_op jit(solution)/shard_map/ppermute | solution.py:30
  263.4 25.8 %collective-permute-start.42 = (f32[384,384]{1,0:T(8,128)S(1)}, f32[384,384]{1,0:T(8,128)S(1)}, u32[]{:S(2)}, u32[]{:S(2)}) collective-permute-start(f32[384,384]{1,0:T(8,128)S(1)} %collective-permute-done.34.refs_6_), channel_id=1, source_target_pairs={{0,8},{1,9},{2,10},{3,11},{4,12},{5,13},{6,14},{7,15},{8,0},{9,1},... | collective-permute-start | bytes 1769480 | tf_op jit(solution)/shard_map/ppermute | solution.py:30
  263.9 25.3 %collective-permute-start.41 = (f32[384,384]{1,0:T(8,128)S(1)}, f32[384,384]{1,0:T(8,128)S(1)}, u32[]{:S(2)}, u32[]{:S(2)}) collective-permute-start(f32[384,384]{1,0:T(8,128)S(1)} %collective-permute-done.33.refs_5_), channel_id=1, source_target_pairs={{0,8},{1,9},{2,10},{3,11},{4,12},{5,13},{6,14},{7,15},{8,0},{9,1},... | collective-permute-start | bytes 1769480 | tf_op jit(solution)/shard_map/ppermute | solution.py:30
  (31 other events, 837.1 us)
